TPU v7x, 32 devices: a whole 2x2x4 slice. The times are simulated.
32 devices in a mesh: wide: 16 (over z, y, x), narrow: 2 (over core).
Axes of the slice: x: 2, y: 2, z: 4, core: 2. Of those that a mesh axis runs over, the one named last changes fastest.
Arguments:
- plan_logits: float32 [2, 2, 2, 32, 1024], P(None, 'narrow'), may hold values from 0 to 3
- pot_size: float32 [2, 2], P('narrow'), may hold values from 0.5 to 2
- payoff_tiles: bfloat16 [32, 1024, 1024], P(('wide', 'narrow')), may hold values from -0.046875 to 0.046875
- parent_first: int32 [32], P(('wide', 'narrow')), may hold values from 0 to 1
- parent_second: int32 [32], P(('wide', 'narrow')), may hold values from 0 to 1
Outputs:
- new_logits: float32 [2, 2, 2, 32, 1024], P(None, 'narrow')
- line_utility: float32 [2, 2, 32, 1024], replicated
All inputs are finite; a program needn't handle non-finite values.
Results may differ from a plain program's by a relative error of at most 0.0031.
Values may be sent and summed in bfloat16 or wider, within the bound.
A program may use at most 64 MiB of HBM per device.

v0:
```python
import jax
import jax.numpy as jnp
from jax import lax
from jax.sharding import PartitionSpec as P

STEPS = 3


learning_rate = 1.0


def per_device(plan_logits, pot_size, payoff_tiles, parent_first, parent_second):
    logits = plan_logits
    line_count = logits.shape[2]
    level_index = lax.axis_index("narrow")
    line_ids = jnp.arange(line_count, dtype=jnp.int32)[None, :]
    pick_first = (parent_first[:, None] == line_ids).astype(jnp.bfloat16)
    pick_second = (parent_second[:, None] == line_ids).astype(jnp.bfloat16)
    sum_first = pick_first.astype(jnp.float32)
    sum_second = pick_second.astype(jnp.float32)
    previous = None
    utility = None
    for iteration in range(STEPS):
        keep = jax.nn.log_sigmoid(logits)
        local_keep = None
        local_fold = None
        every_logit, every_pot = (
            lax.all_gather(logits, "narrow", axis=1, tiled=True),
            lax.all_gather(pot_size, "narrow", axis=0, tiled=True),
        )
        every_keep = jax.nn.log_sigmoid(every_logit)
        every_prefix = jnp.cumsum(every_keep, axis=1) - every_keep
        reached = jnp.exp(jnp.sum(every_keep, axis=1)).astype(jnp.bfloat16)
        every_mass = jnp.mean(jnp.exp(every_prefix), axis=4)[::-1]
        every_fold = (-every_pot[None, :, :, None] * every_mass)[..., None]
        every_log_fold = jax.nn.log_sigmoid(-every_logit) + learning_rate * every_fold
        fold_value = lax.dynamic_slice_in_dim(every_fold, level_index, 1, 1)
        level_count = every_keep.shape[1]
        acc_keep = jnp.zeros_like(keep[:, 0])
        acc_fold = jnp.full_like(keep[:, 0], -jnp.inf)
        local_keep = jnp.zeros_like(keep[:, 0])
        local_fold = jnp.zeros_like(keep[:, 0])
        for level in range(level_count - 1, -1, -1):
            mine = level_index == level
            local_keep = jnp.where(mine, acc_keep, local_keep)
            local_fold = jnp.where(mine, acc_fold, local_fold)
            acc_fold = jnp.logaddexp(every_keep[:, level] + acc_fold, every_log_fold[:, level])
            acc_keep = every_keep[:, level] + acc_keep
        local_keep = local_keep[:, None]
        local_fold = local_fold[:, None]
        first_reach = jnp.einsum(
            "ls,sbj->lbj", pick_first, reached[0], preferred_element_type=jnp.float32
        ).astype(jnp.bfloat16)
        second_reach = jnp.einsum(
            "ls,sbj->lbj", pick_second, reached[1], preferred_element_type=jnp.float32
        ).astype(jnp.bfloat16)
        value_first = jnp.einsum(
            "lbj,lij->lbi", second_reach, payoff_tiles, preferred_element_type=jnp.float32
        )
        value_second = -jnp.einsum(
            "lbi,lij->lbj", first_reach, payoff_tiles, preferred_element_type=jnp.float32
        )
        local_sums = jnp.stack(
            [
                jnp.einsum("ls,lbi->sbi", sum_first, value_first, precision=lax.Precision.HIGHEST),
                jnp.einsum(
                    "ls,lbi->sbi", sum_second, value_second, precision=lax.Precision.HIGHEST
                ),
            ]
        )
        suffix_keep, suffix_fold = (local_keep, local_fold)
        utility = lax.psum(local_sums, ("wide", "narrow"))
        if previous is None:
            previous = utility
        target = 2.0 * utility - previous
        previous = utility
        next_value = (
            jnp.logaddexp(suffix_keep + learning_rate * target[:, None], suffix_fold)
            / learning_rate
        )
        logits = logits + learning_rate * (next_value - fold_value)
    return (logits, utility)


def solution(mesh):
    in_specs = (
        P(None, "narrow", None, None, None),
        P("narrow", None),
        P(("wide", "narrow"), None, None),
        P(("wide", "narrow")),
        P(("wide", "narrow")),
    )
    out_specs = (P(None, "narrow", None, None, None), P())
    return jax.shard_map(
        per_device, mesh=mesh, in_specs=in_specs, out_specs=out_specs, check_vma=False
    )
```

profile of v0, /device:TPU:1, one launch (start us, length us, event | category | flops | bytes accessed | tf_op | source)
XLA Modules:
  0.0 460.5 jit_solution(8445517225513006323)
XLA Ops:
  7.2 0.7 all-gather.5.cloned.1.call-update
  8.0 1.9 all-gather
  11.2 9.9 %all-gather.5.cloned.1.call-done = f32[2,2,2,32,1024]{4,3,2,0,1:T(8,128)} async-done(((f32[2,1,2,32,1024]{4,3,2,0,1:T(8,128)}), f32[2,2,2,32,1024]{4,3,2,0,1:T(8,128)}) %all-gather.5.cloned.1.call-update) | async-done | bytes 1048592 | tf_op jit(solution)/shard_map/all_gather | solution.py:28
  21.1 3.3 fusion.48
  24.4 0.1 exponential_convert_fusion.2
  24.5 0.3 fusion.63
  24.8 0.7 fusion.10
  25.5 0.3 fusion.61
  25.8 0.5 fusion.15
  26.3 0.1 multiply_bitcast_fusion.4
  26.4 0.8 pad_maximum_fusion
  27.3 0.0 all-gather.7.cloned.1.call-start
  27.3 0.9 fusion.68
  28.2 0.1 reverse_multiply_fusion.2
  28.3 126.9 %all-reduce.4.cloned.1.call-done = f32[2,2,32,1024]{3,2,1,0:T(8,128)} async-done(((f32[2,2,32,1024]{3,2,1,0:T(8,128)}), f32[2,2,32,1024]{3,2,1,0:T(8,128)}) %all-reduce.4.cloned.1.call-update) | async-done | bytes 524304 | tf_op jit(solution)/shard_map/psum | solution.py:72
  155.2 3.4 bitcast_add_fusion.6
  158.6 0.0 all-reduce.6.cloned.1.call-start
  158.7 9.3 %all-gather.7.cloned.1.call-done = f32[2,2,2,32,1024]{4,3,2,0,1:T(8,128)} async-done(((f32[2,1,2,32,1024]{4,3,2,0,1:T(8,128)}), f32[2,2,2,32,1024]{4,3,2,0,1:T(8,128)}) %all-gather.7.cloned.1.call-update) | async-done | bytes 1048592 | tf_op jit(solution)/shard_map/all_gather | solution.py:28
  168.0 3.3 fusion.50
  171.4 0.1 exponential_convert_fusion.1
  171.5 0.3 fusion.59
  171.8 0.7 fusion.6
  172.5 0.1 multiply_bitcast_fusion.3
  172.6 0.3 fusion.57
  172.9 0.5 fusion.18
  173.4 0.1 multiply_bitcast_fusion.2
  173.4 0.8 pad_maximum_fusion.1
  174.3 0.0 all-gather.9.cloned.1.call-start
  174.4 3.5 fusion.69
  177.9 0.1 reverse_multiply_fusion.1
  177.9 124.4 %all-reduce.6.cloned.1.call-done = f32[2,2,32,1024]{3,2,1,0:T(8,128)} async-done(((f32[2,2,32,1024]{3,2,1,0:T(8,128)}), f32[2,2,32,1024]{3,2,1,0:T(8,128)}) %all-reduce.6.cloned.1.call-update) | async-done | bytes 524304 | tf_op jit(solution)/shard_map/psum | solution.py:72
  302.4 3.4 bitcast_add_fusion.3
  305.8 0.2 all-reduce.8.cloned.1.call-start
  306.1 9.2 %all-gather.9.cloned.1.call-done = f32[2,2,2,32,1024]{4,3,2,0,1:T(8,128)} async-done(((f32[2,1,2,32,1024]{4,3,2,0,1:T(8,128)}), f32[2,2,2,32,1024]{4,3,2,0,1:T(8,128)}) %all-gather.9.cloned.1.call-update) | async-done | bytes 1048592 | tf_op jit(solution)/shard_map/all_gather | solution.py:28
  315.2 3.3 fusion.52
  318.5 0.1 exponential_convert_fusion
  318.6 0.3 fusion.55
  318.9 0.7 fusion.2
  319.7 0.1 multiply_bitcast_fusion.1
  319.8 0.3 fusion.53
  320.1 0.5 fusion.21
  320.5 0.1 multiply_bitcast_fusion
  320.6 0.8 pad_maximum_fusion.2
  321.5 3.5 fusion.70
  325.0 0.1 reverse_multiply_fusion
  325.1 124.3 %all-reduce.8.cloned.1.call-done = f32[2,2,32,1024]{3,2,1,0:T(8,128)} async-done(((f32[2,2,32,1024]{3,2,1,0:T(8,128)}), f32[2,2,32,1024]{3,2,1,0:T(8,128)}) %all-reduce.8.cloned.1.call-update) | async-done | bytes 524304 | tf_op jit(solution)/shard_map/psum | solution.py:72
  449.4 3.5 fusion.37
  452.9 0.8 copy.54
  (30 shorter events, 0.3 us)
Async XLA Ops:
  7.2 17.6 %copy-start = (bf16[1,1024,1024]{2,1,0:T(8,128)(2,1)S(1)}, bf16[1,1024,1024]{2,1,0:T(8,128)(2,1)}, u32[]{:S(2)}) copy-start(bf16[1,1024,1024]{2,1,0:T(8,128)(2,1)} %param.7) | copy-start | bytes 6291460
  7.2 13.9 %all-gather.5.cloned.1.call-start = ((), (), s32[]{:S(2)}) async-start(), calls=%async_computation | async-start | bytes 1572864 | tf_op jit(solution)/shard_map/all_gather | solution.py:28
  7.9 147.3 %all-reduce.4.cloned.1.call-start = ((), (), s32[]{:S(2)}) async-start(), calls=%async_computation.1 | async-start | bytes 1048576 | tf_op jit(solution)/shard_map/psum | solution.py:72
  25.8 1.5 copy-start.3
  27.3 140.7 %all-gather.7.cloned.1.call-start = ((), (), s32[]{:S(2)}) async-start(), calls=%async_computation.2 | async-start | bytes 1572864 | tf_op jit(solution)/shard_map/all_gather | solution.py:28
  158.6 143.7 %all-reduce.6.cloned.1.call-start = ((), (), s32[]{:S(2)}) async-start(), calls=%async_computation.3 | async-start | bytes 1048576 | tf_op jit(solution)/shard_map/psum | solution.py:72
  173.3 129.1 %copy-start.2 = (f32[2,1,2,32,1024]{4,3,2,0,1:T(8,128)S(1)}, f32[2,1,2,32,1024]{4,3,2,0,1:T(8,128)}, u32[]{:S(2)}) copy-start(f32[2,1,2,32,1024]{4,3,2,0,1:T(8,128)} %bitcast_add_fusion.6) | copy-start | bytes 1572868
  173.3 129.0 %copy-start.6 = (f32[2,2,32,1024]{3,2,1,0:T(8,128)S(1)}, f32[2,2,32,1024]{3,2,1,0:T(8,128)}, u32[]{:S(2)}) copy-start(f32[2,2,32,1024]{3,2,1,0:T(8,128)} %all-reduce.4.cloned.1.call-done) | copy-start | bytes 1572868
  174.3 140.9 %all-gather.9.cloned.1.call-start = ((), (), s32[]{:S(2)}) async-start(), calls=%async_computation.4 | async-start | bytes 1572864 | tf_op jit(solution)/shard_map/all_gather | solution.py:28
  305.8 143.6 %all-reduce.8.cloned.1.call-start = ((), (), s32[]{:S(2)}) async-start(), calls=%async_computation.5 | async-start | bytes 1048576 | tf_op jit(solution)/shard_map/psum | solution.py:72
  320.5 128.9 %copy-start.1 = (f32[2,1,2,32,1024]{4,3,2,0,1:T(8,128)S(1)}, f32[2,1,2,32,1024]{4,3,2,0,1:T(8,128)}, u32[]{:S(2)}) copy-start(f32[2,1,2,32,1024]{4,3,2,0,1:T(8,128)} %bitcast_add_fusion.3) | copy-start | bytes 1572868
  320.5 128.9 %copy-start.4 = (f32[2,2,32,1024]{3,2,1,0:T(8,128)S(1)}, f32[2,2,32,1024]{3,2,1,0:T(8,128)}, u32[]{:S(2)}) copy-start(f32[2,2,32,1024]{3,2,1,0:T(8,128)} %all-reduce.6.cloned.1.call-done) | copy-start | bytes 1572868
  449.4 3.5 copy-start.5
Sparse Core Ops, SparseCore 0:
  9.6 11.4 all-gather.4
  27.4 127.7 all-reduce.3
  158.8 9.2 all-gather.6
  174.6 127.7 all-reduce.5
  305.9 9.2 all-gather.8
  321.6 127.7 all-reduce.7
where the time goes:
time: 462 us; the launch traced here: 461 us
  waiting for transfers between devices  405 us (88%)
  other arithmetic  31.6 us (7%)
  between operations  15.6 us (3%)
  matrix products  5.26 us (1%)
    psum x3, waiting for transfers between devices, per_device(): utility = lax.psum(local_sums, ('wide', 'narrow'))  376 us
    all_gather x3, waiting for transfers between devices, per_device(): lax.all_gather(logits, 'narrow', axis=1, tiled=True)  28.4 us
    neg x3, other arithmetic, per_device(): every_keep = jax.nn.log_sigmoid(every_logit)  9.95 us
  transfers between devices with their start and end apart: 6, of which 6 were waited for; matrix products, arithmetic and copies ran while one was open for 2% of the time, Pallas kernels for 0%

commit v1 on v0

--- a/solution.py
+++ b/solution.py
@@ -1,9 +1,16 @@
+import functools
+
 import jax
 import jax.numpy as jnp
 from jax import lax
+from jax.experimental import pallas as pl
+from jax.experimental.pallas import tpu as pltpu
 from jax.sharding import PartitionSpec as P
 
 STEPS = 3
+ROWS = 16
+LANES = 128
+MESH = pl.DeviceIdType.MESH
 
 
 learning_rate = 1.0
@@ -82,6 +89,350 @@
     return (logits, utility)
 
 
+def softplus(x):
+    return jnp.maximum(x, 0.0) + jnp.log(1.0 + jnp.exp(-jnp.abs(x)))
+
+
+def wait_bytes(ref, sem):
+    pltpu.make_async_copy(ref, ref, sem).wait()
+
+
+def solve_kernel(
+    wide,
+    narrow,
+    logits_ref,
+    pot_ref,
+    payoff_ref,
+    first_ref,
+    second_ref,
+    logits_out,
+    utility_out,
+    state,
+    soft,
+    payoff,
+    pots,
+    parent,
+    parents,
+    reach,
+    mass,
+    fold,
+    values,
+    parts,
+    sums,
+    utility,
+    level_sem,
+    level_sent,
+    pot_sem,
+    pot_sent,
+    parent_sem,
+    parent_sent,
+    payoff_sem,
+    parts_sem,
+    parts_sent,
+    sums_sem,
+    sums_sent,
+    out_sem,
+):
+    devices = wide * narrow
+    _, levels, lines, beliefs, buckets = state.shape
+    own_levels = logits_ref.shape[1]
+    halves = beliefs // ROWS
+    tiles = devices // 2
+    my_wide, my_narrow = lax.axis_index("wide"), lax.axis_index("narrow")
+    me = my_wide * narrow + my_narrow
+    my_levels = pl.ds(my_narrow * own_levels, own_levels)
+
+    def at(device):
+        return (lax.div(device, narrow), lax.rem(device, narrow))
+
+    def remote(src, dst, sent, received, device):
+        return pltpu.make_async_remote_copy(
+            src_ref=src,
+            dst_ref=dst,
+            send_sem=sent,
+            recv_sem=received,
+            device_id=device,
+            device_id_type=MESH,
+        )
+
+    pltpu.make_async_copy(logits_ref, state.at[:, my_levels], level_sem).start()
+    pltpu.make_async_copy(payoff_ref.at[0], payoff, payoff_sem).start()
+
+    barrier = pltpu.get_barrier_semaphore()
+
+    @pl.loop(1, devices)
+    def _(step):
+        pl.semaphore_signal(
+            barrier, inc=1, device_id=at(lax.rem(me + step, devices)), device_id_type=MESH
+        )
+
+    parent[0] = jnp.full((1, LANES), first_ref[0], jnp.int32)
+    parent[1] = jnp.full((1, LANES), second_ref[0], jnp.int32)
+    for level in range(own_levels):
+        for line in range(lines):
+            pots[my_narrow * own_levels + level, line] = jnp.broadcast_to(
+                pot_ref[level : level + 1, line : line + 1], (8, LANES)
+            )
+    pl.semaphore_wait(barrier, devices - 1)
+
+    for step in range(1, narrow):
+        peer = (my_wide, lax.rem(my_narrow + step, narrow))
+        remote(logits_ref, state.at[:, my_levels], level_sent, level_sem, peer).start()
+        remote(pots.at[my_levels], pots.at[my_levels], pot_sent, pot_sem, peer).start()
+
+    @pl.loop(1, devices)
+    def _(step):
+        other = lax.rem(me + step, devices)
+        remote(
+            parent.at[lax.rem(other, 2)], parents.at[me], parent_sent, parent_sem, at(other)
+        ).start()
+
+    pltpu.make_async_copy(parent.at[lax.rem(me, 2)], parents.at[me], parent_sem).start()
+
+    def place(tile):
+        half = lax.rem(tile, halves)
+        chunk = lax.div(tile, halves)
+        return (
+            pl.ds(pl.multiple_of(half * ROWS, ROWS), ROWS),
+            pl.ds(pl.multiple_of(chunk * LANES, LANES), LANES),
+        )
+
+    def finish_tile(player, rows, lanes, fresh):
+        chosen = None
+        for line in range(lines):
+            total = None
+            for level in range(levels):
+                logit, plus = fresh[line][level]
+                if level:
+                    mass[player, level, line, rows] += jnp.exp(total)
+                total = logit - plus if total is None else total + (logit - plus)
+            if chosen is None:
+                chosen = total
+            else:
+                picked = jnp.broadcast_to(parent[player], (ROWS, LANES)) == line
+                chosen = jnp.where(picked, total, chosen)
+        reach[player, rows, lanes] = jnp.exp(chosen).astype(jnp.bfloat16)
+
+    def finish_fold():
+        for player in range(2):
+            for line in range(lines):
+                for level in range(levels):
+                    pot = pots[level, line, 0:1, :]
+                    if level:
+                        mean = jnp.sum(
+                            mass[1 - player, level, line], axis=-1, keepdims=True
+                        ) * (1.0 / buckets)
+                        fold[player, level, line] = -(pot * mean)
+                    else:
+                        fold[player, level, line] = jnp.broadcast_to(-pot, (beliefs, LANES))
+
+    def update(step, player, tile, last):
+        rows, lanes = place(tile)
+        unit = 2 * tile + player
+        fresh = []
+        for line in range(lines):
+            now = utility[step, unit, line].astype(jnp.float32)
+            value = now
+            if step:
+                value = 2.0 * now - utility[step - 1, unit, line].astype(jnp.float32)
+            of_line = [None] * levels
+            for level in range(levels - 1, -1, -1):
+                here = (player, level, line, rows, lanes)
+                lost = fold[player, level, line, rows]
+                logit = state[here] + (value - lost)
+                state[here] = logit
+                if level or not last:
+                    plus = softplus(logit)
+                    value = lost + (plus - soft[here])
+                    if not last:
+                        soft[here] = plus
+                        of_line[level] = (logit, plus)
+            fresh.append(of_line)
+            if last:
+                sums_out[player, line, rows, lanes] = now
+        if not last:
+            finish_tile(player, rows, lanes, fresh)
+
+    sums_out = utility_out
+
+    wait_bytes(pots.at[pl.ds(0, levels - own_levels)], pot_sem)
+    wait_bytes(state, level_sem)
+    mass[...] = jnp.zeros_like(mass)
+    for player in range(2):
+
+        @pl.loop(0, tiles)
+        def _(tile):
+            rows, lanes = place(tile)
+            fresh = []
+            for line in range(lines):
+                of_line = []
+                for level in range(levels):
+                    here = (player, level, line, rows, lanes)
+                    logit = state[here]
+                    plus = softplus(logit)
+                    soft[here] = plus
+                    of_line.append((logit, plus))
+                fresh.append(of_line)
+            finish_tile(player, rows, lanes, fresh)
+
+    wait_bytes(payoff, payoff_sem)
+    width = min(256, buckets)
+    for step in range(STEPS):
+        for player in range(2):
+            for begin in range(0, buckets, width):
+                if player == 0:
+                    product = lax.dot_general(
+                        reach[1],
+                        payoff[begin : begin + width, :],
+                        (((1,), (1,)), ((), ())),
+                        preferred_element_type=jnp.float32,
+                    )
+                else:
+                    product = -jnp.dot(
+                        reach[0],
+                        payoff[:, begin : begin + width],
+                        preferred_element_type=jnp.float32,
+                    )
+                product = product.astype(jnp.bfloat16)
+                for column in range(0, width, LANES):
+                    for half in range(halves):
+                        tile = (begin + column) // LANES * halves + half
+                        values[step, 2 * tile + player] = product[
+                            half * ROWS : (half + 1) * ROWS, column : column + LANES
+                        ]
+
+            @pl.loop(0, tiles)
+            def _(index):
+                unit = 2 * lax.rem(lax.div(me, 2) + index, tiles) + player
+
+                @pl.when(unit != me)
+                def _():
+                    remote(
+                        values.at[step, unit],
+                        parts.at[step, me],
+                        parts_sent.at[step],
+                        parts_sem.at[step],
+                        at(unit),
+                    ).start()
+
+                @pl.when(unit == me)
+                def _():
+                    pltpu.make_async_copy(
+                        values.at[step, unit], parts.at[step, me], parts_sem.at[step]
+                    ).start()
+
+        finish_fold()
+        mass[...] = jnp.zeros_like(mass)
+        if step == 0:
+            wait_bytes(parents, parent_sem)
+        wait_bytes(parts.at[step], parts_sem.at[step])
+
+        def add(device, totals):
+            part = parts[step, device].astype(jnp.float32)
+            owner = jnp.broadcast_to(parents[device], (ROWS, LANES))
+            return tuple(
+                total + jnp.where(owner == line, part, 0.0) for line, total in enumerate(totals)
+            )
+
+        zero = jnp.zeros((ROWS, LANES), jnp.float32)
+        totals = lax.fori_loop(0, devices, add, (zero,) * lines, unroll=8)
+        for line in range(lines):
+            sums[step, line] = totals[line].astype(jnp.bfloat16)
+
+        @pl.loop(1, devices)
+        def _(index):
+            other = lax.rem(me + index, devices)
+            remote(
+                sums.at[step],
+                utility.at[step, me],
+                sums_sent.at[step],
+                sums_sem.at[step],
+                at(other),
+            ).start()
+
+        pltpu.make_async_copy(sums.at[step], utility.at[step, me], sums_sem.at[step]).start()
+        wait_bytes(utility.at[step], sums_sem.at[step])
+        for player in range(2):
+
+            @pl.loop(0, tiles)
+            def _(tile):
+                update(step, player, tile, step == STEPS - 1)
+
+    out = pltpu.make_async_copy(state.at[:, my_levels], logits_out, out_sem)
+    out.start()
+    for _ in range(1, narrow):
+        wait_bytes(state.at[:, my_levels], level_sent)
+        wait_bytes(pots.at[my_levels], pot_sent)
+    wait_bytes(parents.at[pl.ds(0, devices - 1)], parent_sent)
+    for step in range(STEPS):
+        wait_bytes(values.at[step, pl.ds(0, devices - 1)], parts_sent.at[step])
+        wait_bytes(utility.at[step, pl.ds(0, devices - 1)], sums_sent.at[step])
+    out.wait()
+
+
+def solve(wide, narrow, plan_logits, pot_size, payoff_tiles, parent_first, parent_second):
+    devices = wide * narrow
+    players, own_levels, lines, beliefs, buckets = plan_logits.shape
+    levels = own_levels * narrow
+    whole = (players, levels, lines, beliefs, buckets)
+    tile = (ROWS, LANES)
+    dma = pltpu.SemaphoreType.DMA
+    return pl.pallas_call(
+        functools.partial(solve_kernel, wide, narrow),
+        out_shape=(
+            jax.ShapeDtypeStruct(plan_logits.shape, jnp.float32),
+            jax.ShapeDtypeStruct((players, lines, beliefs, buckets), jnp.float32),
+        ),
+        in_specs=[
+            pl.BlockSpec(memory_space=pl.ANY),
+            pl.BlockSpec(memory_space=pltpu.VMEM),
+            pl.BlockSpec(memory_space=pl.ANY),
+            pl.BlockSpec(memory_space=pltpu.SMEM),
+            pl.BlockSpec(memory_space=pltpu.SMEM),
+        ],
+        out_specs=(pl.BlockSpec(memory_space=pl.ANY), pl.BlockSpec(memory_space=pltpu.VMEM)),
+        scratch_shapes=[
+            pltpu.VMEM(whole, jnp.float32),
+            pltpu.VMEM(whole, jnp.float32),
+            pltpu.VMEM((buckets, buckets), jnp.bfloat16),
+            pltpu.VMEM((levels, lines, 8, LANES), jnp.float32),
+            pltpu.VMEM((players, 1, LANES), jnp.int32),
+            pltpu.VMEM((devices, 1, LANES), jnp.int32),
+            pltpu.VMEM((players, beliefs, buckets), jnp.bfloat16),
+            pltpu.VMEM((players, levels, lines, beliefs, LANES), jnp.float32),
+            pltpu.VMEM((players, levels, lines, beliefs, LANES), jnp.float32),
+            pltpu.VMEM((STEPS, devices) + tile, jnp.bfloat16),
+            pltpu.VMEM((STEPS, devices) + tile, jnp.bfloat16),
+            pltpu.VMEM((STEPS, lines) + tile, jnp.bfloat16),
+            pltpu.VMEM((STEPS, devices, lines) + tile, jnp.bfloat16),
+            dma,
+            dma,
+            dma,
+            dma,
+            dma,
+            dma,
+            dma,
+            dma((STEPS,)),
+            dma((STEPS,)),
+            dma((STEPS,)),
+            dma((STEPS,)),
+            dma,
+        ],
+        compiler_params=pltpu.CompilerParams(
+            collective_id=0, has_side_effects=True, vmem_limit_bytes=32 * 1024 * 1024
+        ),
+    )(plan_logits, pot_size, payoff_tiles, parent_first, parent_second)
+
+
+def choose(wide, narrow, *arrays):
+    players, _, _, beliefs, buckets = arrays[0].shape
+    units = players * (beliefs // ROWS) * (buckets // LANES)
+    whole_tiles = beliefs % ROWS == 0 and buckets % LANES == 0
+    if whole_tiles and units == wide * narrow and arrays[2].shape[0] == 1 and narrow > 1:
+        return solve(wide, narrow, *arrays)
+    return per_device(*arrays)
+
+
 def solution(mesh):
     in_specs = (
         P(None, "narrow", None, None, None),
@@ -92,5 +443,9 @@
     )
     out_specs = (P(None, "narrow", None, None, None), P())
     return jax.shard_map(
-        per_device, mesh=mesh, in_specs=in_specs, out_specs=out_specs, check_vma=False
+        functools.partial(choose, mesh.shape["wide"], mesh.shape["narrow"]),
+        mesh=mesh,
+        in_specs=in_specs,
+        out_specs=out_specs,
+        check_vma=False,
     )

time: 462 us -> 61.6 us (0.13)
  the two profiles are of different devices: /device:TPU:1 before, /device:TPU:13 now
where the time goes in v1:
time: 61.6 us; the launch traced here: 61.4 us
  Pallas kernels  54.6 us (89%)
  local copies, waits for them, and re-layouts  4.87 us (8%)
  between operations  1.94 us (3%)
    pallas_call x1, Pallas kernels, solve(): pl.pallas_call(functools.partial(solve_kernel, wide, narrow), out_shape=(...  54.6 us
    unnamed x8, local copies, waits for them, and re-layouts  4.87 us

profile of v1, /device:TPU:13, one launch (start us, length us, event | category | flops | bytes accessed | tf_op | source)
XLA Modules:
  0.0 61.4 jit_solution(2510314159787274357)
XLA Ops:
  1.9 0.0 copy-start
  1.9 1.6 %copy-done = bf16[1,1024,1024]{2,1,0:T(8,128)(2,1)S(1)} copy-done((bf16[1,1024,1024]{2,1,0:T(8,128)(2,1)S(1)}, bf16[1,1024,1024]{2,1,0:T(8,128)(2,1)}, u32[]{:S(2)}) %copy-start) | copy-done | bytes 2097176
  3.5 0.0 copy-start.1
  3.5 1.0 %copy-done.1 = f32[2,1,2,32,1024]{4,3,2,1,0:T(8,128)S(1)} copy-done((f32[2,1,2,32,1024]{4,3,2,1,0:T(8,128)S(1)}, f32[2,1,2,32,1024]{4,3,2,1,0:T(8,128)}, u32[]{:S(2)}) %copy-start.1) | copy-done | bytes 524312
  4.6 0.0 copy-start.2
  4.6 0.7 %copy-done.2 = f32[1,2]{1,0:T(1,128)S(1)} copy-done((f32[1,2]{1,0:T(1,128)S(1)}, f32[1,2]{1,0:T(1,128)}, u32[]{:S(2)}) %copy-start.2) | copy-done | bytes 32
  5.2 54.6 %shard_map.68 = (f32[2,1,2,32,1024]{4,3,2,1,0:T(8,128)S(1)}, f32[2,2,32,1024]{3,2,1,0:T(8,128)S(1)}) custom-call(f32[2,1,2,32,1024]{4,3,2,1,0:T(8,128)S(1)} %copy-done.1, f32[1,2]{1,0:T(1,128)S(1)} %copy-done.2, bf16[1,1024,1024]{2,1,0:T(8,128)(2,1)S(1)} %copy-done, s32[1]{0:T(128)S(6)} %copy.9.first_ref, s32[1]{0:T(128)S(6)} %copy.10.second_ref), custom_call_target="tpu_custom_call" | custom-call | tf_op jit(solution)/shard_map/pallas_call | solution.py:380
  59.8 0.8 %copy.11 = f32[2,1,2,32,1024]{4,3,2,1,0:T(8,128)} copy(f32[2,1,2,32,1024]{4,3,2,1,0:T(8,128)S(1)} %get-tuple-element.4) | data formatting | bytes 1048576
  60.6 0.8 %copy.12 = f32[2,2,32,1024]{3,2,1,0:T(8,128)} copy(f32[2,2,32,1024]{3,2,1,0:T(8,128)S(1)} %get-tuple-element.5) | data formatting | bytes 1048576
Async XLA Ops:
  1.9 1.6 %copy-start = (bf16[1,1024,1024]{2,1,0:T(8,128)(2,1)S(1)}, bf16[1,1024,1024]{2,1,0:T(8,128)(2,1)}, u32[]{:S(2)}) copy-start(bf16[1,1024,1024]{2,1,0:T(8,128)(2,1)} %payoff_ref.1) | copy-start | bytes 6291460
  3.5 1.0 %copy-start.1 = (f32[2,1,2,32,1024]{4,3,2,1,0:T(8,128)S(1)}, f32[2,1,2,32,1024]{4,3,2,1,0:T(8,128)}, u32[]{:S(2)}) copy-start(f32[2,1,2,32,1024]{4,3,2,1,0:T(8,128)} %logits_ref.1) | copy-start | bytes 1572868
  4.6 0.7 %copy-start.2 = (f32[1,2]{1,0:T(1,128)S(1)}, f32[1,2]{1,0:T(1,128)}, u32[]{:S(2)}) copy-start(f32[1,2]{1,0:T(1,128)} %pot_ref.1) | copy-start | bytes 28

commit v2 on v1

v2 whole, which is shorter than its diff:
```python
import functools

import jax
import jax.numpy as jnp
from jax import lax
from jax.experimental import pallas as pl
from jax.experimental.pallas import tpu as pltpu
from jax.sharding import PartitionSpec as P

STEPS = 3
ROWS = 16
LANES = 128
SPAN = 256
WIRE = jnp.bfloat16
SCALE = 1.0
MESH = pl.DeviceIdType.MESH


learning_rate = 1.0


def per_device(plan_logits, pot_size, payoff_tiles, parent_first, parent_second):
    logits = plan_logits
    line_count = logits.shape[2]
    level_index = lax.axis_index("narrow")
    line_ids = jnp.arange(line_count, dtype=jnp.int32)[None, :]
    pick_first = (parent_first[:, None] == line_ids).astype(jnp.bfloat16)
    pick_second = (parent_second[:, None] == line_ids).astype(jnp.bfloat16)
    sum_first = pick_first.astype(jnp.float32)
    sum_second = pick_second.astype(jnp.float32)
    previous = None
    utility = None
    for iteration in range(STEPS):
        keep = jax.nn.log_sigmoid(logits)
        local_keep = None
        local_fold = None
        every_logit, every_pot = (
            lax.all_gather(logits, "narrow", axis=1, tiled=True),
            lax.all_gather(pot_size, "narrow", axis=0, tiled=True),
        )
        every_keep = jax.nn.log_sigmoid(every_logit)
        every_prefix = jnp.cumsum(every_keep, axis=1) - every_keep
        reached = jnp.exp(jnp.sum(every_keep, axis=1)).astype(jnp.bfloat16)
        every_mass = jnp.mean(jnp.exp(every_prefix), axis=4)[::-1]
        every_fold = (-every_pot[None, :, :, None] * every_mass)[..., None]
        every_log_fold = jax.nn.log_sigmoid(-every_logit) + learning_rate * every_fold
        fold_value = lax.dynamic_slice_in_dim(every_fold, level_index, 1, 1)
        level_count = every_keep.shape[1]
        acc_keep = jnp.zeros_like(keep[:, 0])
        acc_fold = jnp.full_like(keep[:, 0], -jnp.inf)
        local_keep = jnp.zeros_like(keep[:, 0])
        local_fold = jnp.zeros_like(keep[:, 0])
        for level in range(level_count - 1, -1, -1):
            mine = level_index == level
            local_keep = jnp.where(mine, acc_keep, local_keep)
            local_fold = jnp.where(mine, acc_fold, local_fold)
            acc_fold = jnp.logaddexp(every_keep[:, level] + acc_fold, every_log_fold[:, level])
            acc_keep = every_keep[:, level] + acc_keep
        local_keep = local_keep[:, None]
        local_fold = local_fold[:, None]
        first_reach = jnp.einsum(
            "ls,sbj->lbj", pick_first, reached[0], preferred_element_type=jnp.float32
        ).astype(jnp.bfloat16)
        second_reach = jnp.einsum(
            "ls,sbj->lbj", pick_second, reached[1], preferred_element_type=jnp.float32
        ).astype(jnp.bfloat16)
        value_first = jnp.einsum(
            "lbj,lij->lbi", second_reach, payoff_tiles, preferred_element_type=jnp.float32
        )
        value_second = -jnp.einsum(
            "lbi,lij->lbj", first_reach, payoff_tiles, preferred_element_type=jnp.float32
        )
        local_sums = jnp.stack(
            [
                jnp.einsum("ls,lbi->sbi", sum_first, value_first, precision=lax.Precision.HIGHEST),
                jnp.einsum(
                    "ls,lbi->sbi", sum_second, value_second, precision=lax.Precision.HIGHEST
                ),
            ]
        )
        suffix_keep, suffix_fold = (local_keep, local_fold)
        utility = lax.psum(local_sums, ("wide", "narrow"))
        if previous is None:
            previous = utility
        target = 2.0 * utility - previous
        previous = utility
        next_value = (
            jnp.logaddexp(suffix_keep + learning_rate * target[:, None], suffix_fold)
            / learning_rate
        )
        logits = logits + learning_rate * (next_value - fold_value)
    return (logits, utility)


def softplus(x):
    return jnp.maximum(x, 0.0) + jnp.log(1.0 + jnp.exp(-jnp.abs(x)))


def wait_bytes(ref, sem):
    pltpu.make_async_copy(ref, ref, sem).wait()


def solve_kernel(
    wide,
    logits_ref,
    pot_ref,
    payoff_ref,
    first_ref,
    second_ref,
    logits_out,
    utility_out,
    state,
    soft,
    payoff,
    pots,
    parent,
    parents,
    reach,
    mass,
    fold,
    values,
    parts,
    sums,
    utility,
    shown,
    level_sem,
    level_sent,
    pot_sem,
    pot_sent,
    parent_sem,
    parent_sent,
    payoff_sem,
    parts_sem,
    parts_sent,
    sums_sem,
    sums_sent,
    pass_sem,
    pass_sent,
    out_sem,
):
    narrow = 2
    devices = wide * narrow
    _, levels, lines, beliefs, buckets = state.shape
    own_levels = logits_ref.shape[1]
    halves = beliefs // ROWS
    my_wide, mine = lax.axis_index("wide"), lax.axis_index("narrow")
    other = 1 - mine
    me = my_wide * narrow + mine
    my_levels = pl.ds(mine * own_levels, own_levels)
    span = next(width for width in (SPAN, LANES) if buckets % width == 0)

    def remote(src, dst, sent, received, device):
        return pltpu.make_async_remote_copy(
            src_ref=src,
            dst_ref=dst,
            send_sem=sent,
            recv_sem=received,
            device_id=device,
            device_id_type=MESH,
        )

    def place(tile):
        half = lax.rem(tile, halves)
        chunk = lax.div(tile, halves)
        return (
            pl.ds(pl.multiple_of(half * ROWS, ROWS), ROWS),
            pl.ds(pl.multiple_of(chunk * LANES, LANES), LANES),
        )

    my_rows, my_lanes = place(my_wide)

    load = pltpu.make_async_copy(payoff_ref.at[0], payoff.at[0], payoff_sem)
    load.start()
    pltpu.make_async_copy(logits_ref, state.at[:, my_levels], level_sem).start()

    barrier = pltpu.get_barrier_semaphore()

    @pl.loop(1, devices)
    def _(step):
        device = lax.rem(me + step, devices)
        pl.semaphore_signal(
            barrier,
            inc=1,
            device_id=(lax.div(device, narrow), lax.rem(device, narrow)),
            device_id_type=MESH,
        )

    parent[0] = jnp.full((1, LANES), first_ref[0], jnp.int32)
    parent[1] = jnp.full((1, LANES), second_ref[0], jnp.int32)
    for level in range(own_levels):
        for line in range(lines):
            pots[mine * own_levels + level, line] = jnp.broadcast_to(
                pot_ref[level : level + 1, line : line + 1], (8, LANES)
            )
    mass[...] = jnp.zeros_like(mass)
    pl.semaphore_wait(barrier, devices - 1)

    sibling = (my_wide, other)
    level_copy = remote(logits_ref, state.at[:, my_levels], level_sent, level_sem, sibling)
    level_copy.start()
    pot_copy = remote(pots.at[my_levels], pots.at[my_levels], pot_sent, pot_sem, sibling)
    pot_copy.start()

    @pl.loop(0, wide)
    def _(step):
        w = lax.rem(my_wide + step, wide)
        remote(parent.at[other], parents.at[me], parent_sent, parent_sem, (w, other)).start()

    @pl.loop(1, wide)
    def _(step):
        w = lax.rem(my_wide + step, wide)
        remote(parent.at[mine], parents.at[me], parent_sent, parent_sem, (w, mine)).start()

    pltpu.make_async_copy(parent.at[mine], parents.at[me], parent_sem).start()

    load.wait()
    side = min(256, buckets)
    for row in range(0, buckets, side):
        for column in range(0, buckets, side):
            payoff[1, column : column + side, row : row + side] = payoff[
                0, row : row + side, column : column + side
            ].T
    wait_bytes(pots.at[pl.ds(0, levels - own_levels)], pot_sem)
    wait_bytes(state, level_sem)

    def finish_block(player, lanes, fresh):
        chosen = None
        for line in range(lines):
            total = None
            for level in range(levels):
                logit, plus = fresh[line][level]
                if level:
                    lost = jnp.exp(total)
                    part = lost[:, :LANES]
                    for column in range(LANES, span, LANES):
                        part = part + lost[:, column : column + LANES]
                    mass[player, level, line] += part
                total = logit - plus if total is None else total + (logit - plus)
            if chosen is None:
                chosen = total
            else:
                picked = jnp.broadcast_to(parent[player][:, :1], (beliefs, span)) == line
                chosen = jnp.where(picked, total, chosen)
        reach[player, :, lanes] = jnp.exp(chosen).astype(jnp.bfloat16)

    def finish_fold():
        for player in range(2):
            for line in range(lines):
                for level in range(levels):
                    pot = pots[level, line, 0:1, :]
                    if level:
                        mean = jnp.sum(
                            mass[1 - player, level, line], axis=-1, keepdims=True
                        ) * (1.0 / buckets)
                        fold[player, level, line] = -(pot * mean)
                    else:
                        fold[player, level, line] = jnp.broadcast_to(-pot, (beliefs, LANES))

    def begin(player):
        @pl.loop(0, buckets // span)
        def _(block):
            lanes = pl.ds(pl.multiple_of(block * span, span), span)
            fresh = []
            for line in range(lines):
                of_line = []
                for level in range(levels):
                    logit = state[player, level, line, :, lanes]
                    of_line.append((logit, softplus(logit)))
                fresh.append(of_line)
            for line in range(lines):
                for level in range(levels):
                    soft[player, level, line, :, lanes] = fresh[line][level][1]
            finish_block(player, lanes, fresh)

    def update(step, player):
        last = step == STEPS - 1

        @pl.loop(0, buckets // span)
        def _(block):
            lanes = pl.ds(pl.multiple_of(block * span, span), span)
            old, seen, lost = {}, {}, {}
            for line in range(lines):
                now = utility[step, player, line, :, lanes].astype(jnp.float32) * (1.0 / SCALE)
                seen[line] = now, now
                if step:
                    before = utility[step - 1, player, line, :, lanes].astype(jnp.float32)
                    seen[line] = now, 2.0 * now - before * (1.0 / SCALE)
                for level in range(levels):
                    here = (player, level, line, slice(None), lanes)
                    old[line, level] = state[here], soft[here]
                    lost[line, level] = jnp.concatenate(
                        [fold[player, level, line]] * (span // LANES), axis=1
                    )
            fresh = []
            for line in range(lines):
                value = seen[line][1]
                of_line = [None] * levels
                for level in range(levels - 1, -1, -1):
                    logit = old[line, level][0] + (value - lost[line, level])
                    plus = None
                    if level or not last:
                        plus = softplus(logit)
                        value = lost[line, level] + (plus - old[line, level][1])
                    of_line[level] = logit, plus
                fresh.append(of_line)
            for line in range(lines):
                for level in range(levels):
                    here = (player, level, line, slice(None), lanes)
                    state[here] = fresh[line][level][0]
                    if not last:
                        soft[here] = fresh[line][level][1]
                if last:
                    shown[player, line, :, lanes] = seen[line][0]
            if not last:
                finish_block(player, lanes, fresh)

    def respond(step, player):
        target = 1 - player
        factor = jnp.where(player == 0, -SCALE, SCALE).astype(jnp.float32)
        for start in range(0, buckets, side):
            product = jnp.dot(
                reach[player],
                payoff[player, :, start : start + side],
                preferred_element_type=jnp.float32,
            )
            values[step, target, :, start : start + side] = (product * factor).astype(WIRE)

    def send_part(step, target, w):
        rows, lanes = place(w)
        return (
            values.at[step, target, rows, lanes],
            parts.at[step, me],
            parts_sent.at[step],
            parts_sem.at[step],
            (w, target),
        )

    begin(mine)
    for step in range(STEPS):
        respond(step, mine)

        @pl.loop(0, wide)
        def _(index):
            w = lax.rem(my_wide + index, wide)
            remote(*send_part(step, other, w)).start()

        if step:
            wait_bytes(utility.at[step - 1, other], pass_sem.at[step - 1])
            update(step - 1, other)
        else:
            begin(other)
        respond(step, other)

        @pl.loop(1, wide)
        def _(index):
            w = lax.rem(my_wide + index, wide)
            remote(*send_part(step, mine, w)).start()

        own = values.at[step, mine, my_rows, my_lanes]
        pltpu.make_async_copy(own, parts.at[step, me], parts_sem.at[step]).start()
        finish_fold()
        mass[...] = jnp.zeros_like(mass)
        if step == 0:
            wait_bytes(parents, parent_sem)
        wait_bytes(parts.at[step], parts_sem.at[step])

        def add(device, totals):
            part = parts[step, device].astype(jnp.float32)
            owner = jnp.broadcast_to(parents[device], (ROWS, LANES))
            return tuple(
                total + jnp.where(owner == line, part, 0.0) for line, total in enumerate(totals)
            )

        zero = jnp.zeros((ROWS, LANES), jnp.float32)
        totals = lax.fori_loop(0, devices, add, (zero,) * lines, unroll=8)
        for line in range(lines):
            sums[step, line] = totals[line].astype(WIRE)

        here = utility.at[step, mine, :, my_rows, my_lanes]

        @pl.loop(1, wide)
        def _(index):
            w = lax.rem(my_wide + index, wide)
            remote(
                sums.at[step], here, sums_sent.at[step, index], sums_sem.at[step], (w, mine)
            ).start()

        pltpu.make_async_copy(sums.at[step], here, sums_sem.at[step]).start()
        half = utility.at[step, mine]
        wait_bytes(half, sums_sem.at[step])
        remote(half, half, pass_sent.at[step], pass_sem.at[step], sibling).start()
        update(step, mine)

    final = STEPS - 1
    outs = [
        pltpu.make_async_copy(
            state.at[player, my_levels], logits_out.at[player], out_sem.at[0, index]
        )
        for index, player in enumerate((mine, other))
    ] + [
        pltpu.make_async_copy(shown.at[player], utility_out.at[player], out_sem.at[1, index])
        for index, player in enumerate((mine, other))
    ]
    outs[0].start()
    outs[2].start()
    wait_bytes(utility.at[final, other], pass_sem.at[final])
    update(final, other)
    outs[1].start()
    outs[3].start()
    level_copy.wait_send()
    pot_copy.wait_send()
    wait_bytes(parents.at[pl.ds(0, devices - 1)], parent_sent)
    for step in range(STEPS):
        wait_bytes(parts.at[step, pl.ds(0, devices - 1)], parts_sent.at[step])
        wait_bytes(utility.at[step, mine], pass_sent.at[step])

        @pl.loop(1, wide)
        def _(index):
            wait_bytes(sums.at[step], sums_sent.at[step, index])

    for out in outs:
        out.wait()


def solve(wide, plan_logits, pot_size, payoff_tiles, parent_first, parent_second):
    devices = wide * 2
    players, own_levels, lines, beliefs, buckets = plan_logits.shape
    levels = own_levels * 2
    whole = (players, levels, lines, beliefs, buckets)
    tile = (ROWS, LANES)
    dma = pltpu.SemaphoreType.DMA
    return pl.pallas_call(
        functools.partial(solve_kernel, wide),
        out_shape=(
            jax.ShapeDtypeStruct(plan_logits.shape, jnp.float32),
            jax.ShapeDtypeStruct((players, lines, beliefs, buckets), jnp.float32),
        ),
        in_specs=[
            pl.BlockSpec(memory_space=pltpu.HBM),
            pl.BlockSpec(memory_space=pltpu.VMEM),
            pl.BlockSpec(memory_space=pltpu.HBM),
            pl.BlockSpec(memory_space=pltpu.SMEM),
            pl.BlockSpec(memory_space=pltpu.SMEM),
        ],
        out_specs=(
            pl.BlockSpec(memory_space=pl.ANY),
            pl.BlockSpec(memory_space=pl.ANY),
        ),
        scratch_shapes=[
            pltpu.VMEM(whole, jnp.float32),
            pltpu.VMEM(whole, jnp.float32),
            pltpu.VMEM((2, buckets, buckets), jnp.bfloat16),
            pltpu.VMEM((levels, lines, 8, LANES), jnp.float32),
            pltpu.VMEM((players, 1, LANES), jnp.int32),
            pltpu.VMEM((devices, 1, LANES), jnp.int32),
            pltpu.VMEM((players, beliefs, buckets), jnp.bfloat16),
            pltpu.VMEM((players, levels, lines, beliefs, LANES), jnp.float32),
            pltpu.VMEM((players, levels, lines, beliefs, LANES), jnp.float32),
            pltpu.VMEM((STEPS, players, beliefs, buckets), WIRE),
            pltpu.VMEM((STEPS, devices) + tile, WIRE),
            pltpu.VMEM((STEPS, lines) + tile, WIRE),
            pltpu.VMEM((STEPS, players, lines, beliefs, buckets), WIRE),
            pltpu.VMEM((players, lines, beliefs, buckets), jnp.float32),
            dma,
            dma,
            dma,
            dma,
            dma,
            dma,
            dma,
            dma((STEPS,)),
            dma((STEPS,)),
            dma((STEPS,)),
            dma((STEPS, wide)),
            dma((STEPS,)),
            dma((STEPS,)),
            dma((2, 2)),
        ],
        compiler_params=pltpu.CompilerParams(
            collective_id=0, has_side_effects=True, vmem_limit_bytes=32 * 1024 * 1024
        ),
    )(plan_logits, pot_size, payoff_tiles, parent_first, parent_second)


def choose(wide, narrow, *arrays):
    players, _, _, beliefs, buckets = arrays[0].shape
    units = players * (beliefs // ROWS) * (buckets // LANES)
    whole_tiles = beliefs % ROWS == 0 and buckets % LANES == 0
    if whole_tiles and units == wide * narrow and arrays[2].shape[0] == 1 and narrow == 2:
        return solve(wide, *arrays)
    return per_device(*arrays)


def solution(mesh):
    in_specs = (
        P(None, "narrow", None, None, None),
        P("narrow", None),
        P(("wide", "narrow"), None, None),
        P(("wide", "narrow")),
        P(("wide", "narrow")),
    )
    out_specs = (P(None, "narrow", None, None, None), P())
    return jax.shard_map(
        functools.partial(choose, mesh.shape["wide"], mesh.shape["narrow"]),
        mesh=mesh,
        in_specs=in_specs,
        out_specs=out_specs,
        check_vma=False,
    )
```

time: 61.6 us -> 52.9 us (0.86)
  the two profiles are of different devices: /device:TPU:13 before, /device:TPU:1 now
where the time goes in v2:
time: 52.9 us; the launch traced here: 52.7 us
  Pallas kernels  45.9 us (87%)
  local copies, waits for them, and re-layouts  4.87 us (9%)
  between operations  1.94 us (4%)
    pallas_call x1, Pallas kernels, solve(): pl.pallas_call(functools.partial(solve_kernel, wide), out_shape=(jax.Shap...  45.9 us
    unnamed x8, local copies, waits for them, and re-layouts  4.87 us

profile of v2, /device:TPU:1, one launch (start us, length us, event | category | flops | bytes accessed | tf_op | source)
XLA Modules:
  0.0 52.7 jit_solution(12620907557051232566)
XLA Ops:
  1.9 0.0 copy-start
  1.9 1.6 %copy-done = bf16[1,1024,1024]{2,1,0:T(8,128)(2,1)S(1)} copy-done((bf16[1,1024,1024]{2,1,0:T(8,128)(2,1)S(1)}, bf16[1,1024,1024]{2,1,0:T(8,128)(2,1)}, u32[]{:S(2)}) %copy-start) | copy-done | bytes 2097176
  3.5 0.0 copy-start.1
  3.5 1.0 %copy-done.1 = f32[2,1,2,32,1024]{4,3,2,1,0:T(8,128)S(1)} copy-done((f32[2,1,2,32,1024]{4,3,2,1,0:T(8,128)S(1)}, f32[2,1,2,32,1024]{4,3,2,1,0:T(8,128)}, u32[]{:S(2)}) %copy-start.1) | copy-done | bytes 524312
  4.6 0.0 copy-start.2
  4.6 0.7 %copy-done.2 = f32[1,2]{1,0:T(1,128)S(1)} copy-done((f32[1,2]{1,0:T(1,128)S(1)}, f32[1,2]{1,0:T(1,128)}, u32[]{:S(2)}) %copy-start.2) | copy-done | bytes 32
  5.2 45.9 %shard_map.68 = (f32[2,1,2,32,1024]{4,3,2,1,0:T(8,128)S(1)}, f32[2,2,32,1024]{3,2,1,0:T(8,128)S(1)}) custom-call(f32[2,1,2,32,1024]{4,3,2,1,0:T(8,128)S(1)} %copy-done.1, f32[1,2]{1,0:T(1,128)S(1)} %copy-done.2, bf16[1,1024,1024]{2,1,0:T(8,128)(2,1)S(1)} %copy-done, s32[1]{0:T(128)S(6)} %copy.9.first_ref, s32[1]{0:T(128)S(6)} %copy.10.second_ref), custom_call_target="tpu_custom_call" | custom-call | tf_op jit(solution)/shard_map/pallas_call | solution.py:432
  51.1 0.8 %copy.11 = f32[2,1,2,32,1024]{4,3,2,1,0:T(8,128)} copy(f32[2,1,2,32,1024]{4,3,2,1,0:T(8,128)S(1)} %get-tuple-element.4) | data formatting | bytes 1048576
  51.9 0.8 %copy.12 = f32[2,2,32,1024]{3,2,1,0:T(8,128)} copy(f32[2,2,32,1024]{3,2,1,0:T(8,128)S(1)} %get-tuple-element.5) | data formatting | bytes 1048576
Async XLA Ops:
  1.9 1.6 %copy-start = (bf16[1,1024,1024]{2,1,0:T(8,128)(2,1)S(1)}, bf16[1,1024,1024]{2,1,0:T(8,128)(2,1)}, u32[]{:S(2)}) copy-start(bf16[1,1024,1024]{2,1,0:T(8,128)(2,1)} %payoff_ref.1) | copy-start | bytes 6291460
  3.5 1.0 %copy-start.1 = (f32[2,1,2,32,1024]{4,3,2,1,0:T(8,128)S(1)}, f32[2,1,2,32,1024]{4,3,2,1,0:T(8,128)}, u32[]{:S(2)}) copy-start(f32[2,1,2,32,1024]{4,3,2,1,0:T(8,128)} %logits_ref.1) | copy-start | bytes 1572868
  4.6 0.7 %copy-start.2 = (f32[1,2]{1,0:T(1,128)S(1)}, f32[1,2]{1,0:T(1,128)}, u32[]{:S(2)}) copy-start(f32[1,2]{1,0:T(1,128)} %pot_ref.1) | copy-start | bytes 28

commit v3 on v2

--- a/solution.py
+++ b/solution.py
@@ -123,6 +123,7 @@
     sums,
     utility,
     shown,
+    running,
     level_sem,
     level_sent,
     pot_sem,
@@ -168,10 +169,23 @@
         )
 
     my_rows, my_lanes = place(my_wide)
+    blocks = buckets // span
+    owners = wide // blocks
+    my_block = lax.div(my_wide, owners)
+    toward = 1 - 2 * lax.rem(my_block, 2)
+
+    def lanes_of(block):
+        return pl.ds(pl.multiple_of(block * span, span), span)
+
+    def nearest(index):
+        return lax.rem(my_block + index * toward + blocks, blocks)
 
     load = pltpu.make_async_copy(payoff_ref.at[0], payoff.at[0], payoff_sem)
     load.start()
-    pltpu.make_async_copy(logits_ref, state.at[:, my_levels], level_sem).start()
+    for player in (mine, other):
+        pltpu.make_async_copy(
+            logits_ref.at[player], state.at[player, my_levels], level_sem.at[player]
+        ).start()
 
     barrier = pltpu.get_barrier_semaphore()
 
@@ -189,29 +203,39 @@
     parent[1] = jnp.full((1, LANES), second_ref[0], jnp.int32)
     for level in range(own_levels):
         for line in range(lines):
-            pots[mine * own_levels + level, line] = jnp.broadcast_to(
-                pot_ref[level : level + 1, line : line + 1], (8, LANES)
+            pots[mine * own_levels + level, line] = jnp.full(
+                (8, LANES), pot_ref[level, line], jnp.float32
             )
     mass[...] = jnp.zeros_like(mass)
     pl.semaphore_wait(barrier, devices - 1)
 
     sibling = (my_wide, other)
-    level_copy = remote(logits_ref, state.at[:, my_levels], level_sent, level_sem, sibling)
-    level_copy.start()
+    level_copies = [
+        remote(
+            logits_ref.at[player],
+            state.at[player, my_levels],
+            level_sent.at[player],
+            level_sem.at[player],
+            sibling,
+        )
+        for player in (other, mine)
+    ]
+    for copy in level_copies:
+        copy.start()
     pot_copy = remote(pots.at[my_levels], pots.at[my_levels], pot_sent, pot_sem, sibling)
     pot_copy.start()
 
     @pl.loop(0, wide)
     def _(step):
         w = lax.rem(my_wide + step, wide)
-        remote(parent.at[other], parents.at[me], parent_sent, parent_sem, (w, other)).start()
+        remote(parent.at[other], parents.at[mine, my_wide], parent_sent, parent_sem, (w, other)).start()
 
     @pl.loop(1, wide)
     def _(step):
         w = lax.rem(my_wide + step, wide)
-        remote(parent.at[mine], parents.at[me], parent_sent, parent_sem, (w, mine)).start()
-
-    pltpu.make_async_copy(parent.at[mine], parents.at[me], parent_sem).start()
+        remote(parent.at[mine], parents.at[mine, my_wide], parent_sent, parent_sem, (w, mine)).start()
+
+    pltpu.make_async_copy(parent.at[mine], parents.at[mine, my_wide], parent_sem).start()
 
     load.wait()
     side = min(256, buckets)
@@ -221,7 +245,6 @@
                 0, row : row + side, column : column + side
             ].T
     wait_bytes(pots.at[pl.ds(0, levels - own_levels)], pot_sem)
-    wait_bytes(state, level_sem)
 
     def finish_block(player, lanes, fresh):
         chosen = None
@@ -256,10 +279,22 @@
                     else:
                         fold[player, level, line] = jnp.broadcast_to(-pot, (beliefs, LANES))
 
+    def respond(player, lanes):
+        width = min(512, buckets)
+        for start in range(0, buckets, width):
+            running[:, start : start + width] += jnp.dot(
+                reach[player, :, lanes],
+                payoff[player, lanes, start : start + width],
+                preferred_element_type=jnp.float32,
+            )
+
     def begin(player):
-        @pl.loop(0, buckets // span)
+        wait_bytes(state.at[player], level_sem.at[player])
+        running[...] = jnp.zeros_like(running)
+
+        @pl.loop(0, blocks)
         def _(block):
-            lanes = pl.ds(pl.multiple_of(block * span, span), span)
+            lanes = lanes_of(block)
             fresh = []
             for line in range(lines):
                 of_line = []
@@ -271,13 +306,24 @@
                 for level in range(levels):
                     soft[player, level, line, :, lanes] = fresh[line][level][1]
             finish_block(player, lanes, fresh)
-
-    def update(step, player):
+            respond(player, lanes)
+
+    def update(step, player, forward):
         last = step == STEPS - 1
-
-        @pl.loop(0, buckets // span)
-        def _(block):
-            lanes = pl.ds(pl.multiple_of(block * span, span), span)
+        running[...] = jnp.zeros_like(running)
+
+        @pl.loop(0, blocks)
+        def _(index):
+            block = nearest(index)
+            lanes = lanes_of(block)
+            arrived = utility.at[step, player, :, :, lanes]
+            if forward:
+                wait_bytes(arrived, sums_sem.at[step, block])
+                remote(
+                    arrived, arrived, pass_sent.at[step, block], pass_sem.at[step, block], sibling
+                ).start()
+            else:
+                wait_bytes(arrived, pass_sem.at[step, block])
             old, seen, lost = {}, {}, {}
             for line in range(lines):
                 now = utility[step, player, line, :, lanes].astype(jnp.float32) * (1.0 / SCALE)
@@ -313,31 +359,26 @@
                     shown[player, line, :, lanes] = seen[line][0]
             if not last:
                 finish_block(player, lanes, fresh)
-
-    def respond(step, player):
+                respond(player, lanes)
+
+    def answer(step, player):
         target = 1 - player
         factor = jnp.where(player == 0, -SCALE, SCALE).astype(jnp.float32)
-        for start in range(0, buckets, side):
-            product = jnp.dot(
-                reach[player],
-                payoff[player, :, start : start + side],
-                preferred_element_type=jnp.float32,
-            )
-            values[step, target, :, start : start + side] = (product * factor).astype(WIRE)
+        values[step, target] = (running[...] * factor).astype(WIRE)
 
     def send_part(step, target, w):
         rows, lanes = place(w)
         return (
             values.at[step, target, rows, lanes],
-            parts.at[step, me],
+            parts.at[step, mine, my_wide],
             parts_sent.at[step],
-            parts_sem.at[step],
+            parts_sem.at[step, mine],
             (w, target),
         )
 
     begin(mine)
     for step in range(STEPS):
-        respond(step, mine)
+        answer(step, mine)
 
         @pl.loop(0, wide)
         def _(index):
@@ -345,11 +386,10 @@
             remote(*send_part(step, other, w)).start()
 
         if step:
-            wait_bytes(utility.at[step - 1, other], pass_sem.at[step - 1])
-            update(step - 1, other)
+            update(step - 1, other, False)
         else:
             begin(other)
-        respond(step, other)
+        answer(step, other)
 
         @pl.loop(1, wide)
         def _(index):
@@ -357,22 +397,26 @@
             remote(*send_part(step, mine, w)).start()
 
         own = values.at[step, mine, my_rows, my_lanes]
-        pltpu.make_async_copy(own, parts.at[step, me], parts_sem.at[step]).start()
+        pltpu.make_async_copy(
+            own, parts.at[step, mine, my_wide], parts_sem.at[step, mine]
+        ).start()
         finish_fold()
         mass[...] = jnp.zeros_like(mass)
         if step == 0:
             wait_bytes(parents, parent_sem)
-        wait_bytes(parts.at[step], parts_sem.at[step])
-
-        def add(device, totals):
-            part = parts[step, device].astype(jnp.float32)
-            owner = jnp.broadcast_to(parents[device], (ROWS, LANES))
-            return tuple(
-                total + jnp.where(owner == line, part, 0.0) for line, total in enumerate(totals)
-            )
-
-        zero = jnp.zeros((ROWS, LANES), jnp.float32)
-        totals = lax.fori_loop(0, devices, add, (zero,) * lines, unroll=8)
+        totals = (jnp.zeros((ROWS, LANES), jnp.float32),) * lines
+        for core in (other, mine):
+            wait_bytes(parts.at[step, core], parts_sem.at[step, core])
+
+            def add(w, totals):
+                part = parts[step, core, w].astype(jnp.float32)
+                owner = jnp.broadcast_to(parents[core, w], (ROWS, LANES))
+                return tuple(
+                    total + jnp.where(owner == line, part, 0.0)
+                    for line, total in enumerate(totals)
+                )
+
+            totals = lax.fori_loop(0, wide, add, totals, unroll=8)
         for line in range(lines):
             sums[step, line] = totals[line].astype(WIRE)
 
@@ -380,16 +424,13 @@
 
         @pl.loop(1, wide)
         def _(index):
-            w = lax.rem(my_wide + index, wide)
+            w = lax.rem(my_wide + index * toward + wide, wide)
             remote(
-                sums.at[step], here, sums_sent.at[step, index], sums_sem.at[step], (w, mine)
+                sums.at[step], here, sums_sent.at[step, index], sums_sem.at[step, my_block], (w, mine)
             ).start()
 
-        pltpu.make_async_copy(sums.at[step], here, sums_sem.at[step]).start()
-        half = utility.at[step, mine]
-        wait_bytes(half, sums_sem.at[step])
-        remote(half, half, pass_sent.at[step], pass_sem.at[step], sibling).start()
-        update(step, mine)
+        pltpu.make_async_copy(sums.at[step], here, sums_sem.at[step, my_block]).start()
+        update(step, mine, True)
 
     final = STEPS - 1
     outs = [
@@ -403,16 +444,21 @@
     ]
     outs[0].start()
     outs[2].start()
-    wait_bytes(utility.at[final, other], pass_sem.at[final])
-    update(final, other)
+    update(final, other, False)
     outs[1].start()
     outs[3].start()
-    level_copy.wait_send()
+    for copy in level_copies:
+        copy.wait_send()
     pot_copy.wait_send()
-    wait_bytes(parents.at[pl.ds(0, devices - 1)], parent_sent)
+    for core, count in enumerate((wide, wide - 1)):
+        wait_bytes(parents.at[core, pl.ds(0, count)], parent_sent)
     for step in range(STEPS):
-        wait_bytes(parts.at[step, pl.ds(0, devices - 1)], parts_sent.at[step])
-        wait_bytes(utility.at[step, mine], pass_sent.at[step])
+        for core, count in enumerate((wide, wide - 1)):
+            wait_bytes(parts.at[step, core, pl.ds(0, count)], parts_sent.at[step])
+
+        @pl.loop(0, blocks)
+        def _(block):
+            wait_bytes(utility.at[step, mine, :, :, lanes_of(block)], pass_sent.at[step, block])
 
         @pl.loop(1, wide)
         def _(index):
@@ -428,6 +474,7 @@
     levels = own_levels * 2
     whole = (players, levels, lines, beliefs, buckets)
     tile = (ROWS, LANES)
+    blocks = buckets // next(width for width in (SPAN, LANES) if buckets % width == 0)
     dma = pltpu.SemaphoreType.DMA
     return pl.pallas_call(
         functools.partial(solve_kernel, wide),
@@ -437,7 +484,7 @@
         ),
         in_specs=[
             pl.BlockSpec(memory_space=pltpu.HBM),
-            pl.BlockSpec(memory_space=pltpu.VMEM),
+            pl.BlockSpec(memory_space=pltpu.SMEM),
             pl.BlockSpec(memory_space=pltpu.HBM),
             pl.BlockSpec(memory_space=pltpu.SMEM),
             pl.BlockSpec(memory_space=pltpu.SMEM),
@@ -452,32 +499,33 @@
             pltpu.VMEM((2, buckets, buckets), jnp.bfloat16),
             pltpu.VMEM((levels, lines, 8, LANES), jnp.float32),
             pltpu.VMEM((players, 1, LANES), jnp.int32),
-            pltpu.VMEM((devices, 1, LANES), jnp.int32),
+            pltpu.VMEM((2, wide, 1, LANES), jnp.int32),
             pltpu.VMEM((players, beliefs, buckets), jnp.bfloat16),
             pltpu.VMEM((players, levels, lines, beliefs, LANES), jnp.float32),
             pltpu.VMEM((players, levels, lines, beliefs, LANES), jnp.float32),
             pltpu.VMEM((STEPS, players, beliefs, buckets), WIRE),
-            pltpu.VMEM((STEPS, devices) + tile, WIRE),
+            pltpu.VMEM((STEPS, 2, wide) + tile, WIRE),
             pltpu.VMEM((STEPS, lines) + tile, WIRE),
             pltpu.VMEM((STEPS, players, lines, beliefs, buckets), WIRE),
             pltpu.VMEM((players, lines, beliefs, buckets), jnp.float32),
+            pltpu.VMEM((beliefs, buckets), jnp.float32),
+            dma((2,)),
+            dma((2,)),
             dma,
             dma,
             dma,
             dma,
             dma,
-            dma,
-            dma,
+            dma((STEPS, 2)),
             dma((STEPS,)),
-            dma((STEPS,)),
-            dma((STEPS,)),
+            dma((STEPS, blocks)),
             dma((STEPS, wide)),
-            dma((STEPS,)),
-            dma((STEPS,)),
+            dma((STEPS, blocks)),
+            dma((STEPS, blocks)),
             dma((2, 2)),
         ],
         compiler_params=pltpu.CompilerParams(
-            collective_id=0, has_side_effects=True, vmem_limit_bytes=32 * 1024 * 1024
+            collective_id=0, has_side_effects=True, vmem_limit_bytes=60 * 1024 * 1024
         ),
     )(plan_logits, pot_size, payoff_tiles, parent_first, parent_second)
 

time: 52.9 us -> 54.8 us (1.036)
  Pallas kernels: 45.9 us -> 48.8 us
  local copies, waits for them, and re-layouts: 4.87 us -> 3.77 us
    pallas_call x1, Pallas kernels: 45.9 us -> 48.8 us  [solve(): pl.pallas_call(functools.partial(solve_kernel, wide), out_shape=(jax.Shap...]
    unnamed x8 -> x2, local copies, waits for them, and re-layouts: 4.87 us -> 3.77 us
where the time goes in v3:
time: 54.8 us; the launch traced here: 54.5 us
  Pallas kernels  48.8 us (89%)
  local copies, waits for them, and re-layouts  3.77 us (7%)
  between operations  1.93 us (4%)
    pallas_call x1, Pallas kernels, solve(): pl.pallas_call(functools.partial(solve_kernel, wide), out_shape=(jax.Shap...  48.8 us
    unnamed x2, local copies, waits for them, and re-layouts  3.77 us

profile of v3, /device:TPU:1, one launch (start us, length us, event | category | flops | bytes accessed | tf_op | source)
XLA Modules:
  0.0 54.5 jit_solution(7686967645220666748)
XLA Ops:
  1.9 48.8 %shard_map.68 = (f32[2,1,2,32,1024]{4,3,2,1,0:T(8,128)}, f32[2,2,32,1024]{3,2,1,0:T(8,128)}) custom-call(f32[2,1,2,32,1024]{4,3,2,1,0:T(8,128)} %logits_ref.1, f32[1,2]{1,0:T(1,128)} %pot_ref.1, bf16[1,1024,1024]{2,1,0:T(8,128)(2,1)} %payoff_ref.1, s32[1]{0:T(128)S(6)} %copy.9.first_ref, s32[1]{0:T(128)S(6)} %copy.10.second_ref), custom_call_target="tpu_custom_call" | custom-call | tf_op jit(solution)/shard_map/pallas_call | solution.py:479
  50.8 1.9 %copy.11 = f32[2,1,2,32,1024]{4,3,2,1,0:T(8,128)} copy(f32[2,1,2,32,1024]{4,3,2,1,0:T(8,128)} %get-tuple-element.4) | data formatting | bytes 1048576
  52.7 1.9 %copy.12 = f32[2,2,32,1024]{3,2,1,0:T(8,128)} copy(f32[2,2,32,1024]{3,2,1,0:T(8,128)} %get-tuple-element.5) | data formatting | bytes 1048576

commit v4 on v3

--- a/solution.py
+++ b/solution.py
@@ -120,6 +120,8 @@
     fold,
     values,
     parts,
+    partial,
+    gathered,
     sums,
     utility,
     shown,
@@ -133,6 +135,8 @@
     payoff_sem,
     parts_sem,
     parts_sent,
+    partial_sem,
+    partial_sent,
     sums_sem,
     sums_sent,
     pass_sem,
@@ -160,25 +164,26 @@
             device_id_type=MESH,
         )
 
-    def place(tile):
-        half = lax.rem(tile, halves)
-        chunk = lax.div(tile, halves)
-        return (
-            pl.ds(pl.multiple_of(half * ROWS, ROWS), ROWS),
-            pl.ds(pl.multiple_of(chunk * LANES, LANES), LANES),
-        )
-
-    my_rows, my_lanes = place(my_wide)
     blocks = buckets // span
     owners = wide // blocks
-    my_block = lax.div(my_wide, owners)
-    toward = 1 - 2 * lax.rem(my_block, 2)
+    my_block, my_row = lax.rem(my_wide, blocks), lax.div(my_wide, blocks)
+
+    def across(step):
+        return my_row * blocks + lax.rem(my_block + step, blocks)
+
+    def along(step):
+        return lax.rem(my_wide + step * blocks, wide)
+
+    my_rows = pl.ds(pl.multiple_of(lax.rem(my_row, halves) * ROWS, ROWS), ROWS)
+    my_lanes = pl.ds(
+        pl.multiple_of(my_block * span + lax.div(my_row, halves) * LANES, LANES), LANES
+    )
 
     def lanes_of(block):
         return pl.ds(pl.multiple_of(block * span, span), span)
 
     def nearest(index):
-        return lax.rem(my_block + index * toward + blocks, blocks)
+        return lax.rem(my_block + index, blocks)
 
     load = pltpu.make_async_copy(payoff_ref.at[0], payoff.at[0], payoff_sem)
     load.start()
@@ -189,15 +194,15 @@
 
     barrier = pltpu.get_barrier_semaphore()
 
-    @pl.loop(1, devices)
-    def _(step):
-        device = lax.rem(me + step, devices)
-        pl.semaphore_signal(
-            barrier,
-            inc=1,
-            device_id=(lax.div(device, narrow), lax.rem(device, narrow)),
-            device_id_type=MESH,
-        )
+    def greet(device):
+        pl.semaphore_signal(barrier, inc=1, device_id=device, device_id_type=MESH)
+
+    for step in range(blocks):
+        greet((across(step), other))
+        if step:
+            greet((across(step), mine))
+    for step in range(1, owners):
+        greet((along(step), mine))
 
     parent[0] = jnp.full((1, LANES), first_ref[0], jnp.int32)
     parent[1] = jnp.full((1, LANES), second_ref[0], jnp.int32)
@@ -207,7 +212,7 @@
                 (8, LANES), pot_ref[level, line], jnp.float32
             )
     mass[...] = jnp.zeros_like(mass)
-    pl.semaphore_wait(barrier, devices - 1)
+    pl.semaphore_wait(barrier, 2 * blocks - 1 + owners - 1)
 
     sibling = (my_wide, other)
     level_copies = [
@@ -225,17 +230,16 @@
     pot_copy = remote(pots.at[my_levels], pots.at[my_levels], pot_sent, pot_sem, sibling)
     pot_copy.start()
 
-    @pl.loop(0, wide)
-    def _(step):
-        w = lax.rem(my_wide + step, wide)
-        remote(parent.at[other], parents.at[mine, my_wide], parent_sent, parent_sem, (w, other)).start()
-
-    @pl.loop(1, wide)
-    def _(step):
-        w = lax.rem(my_wide + step, wide)
-        remote(parent.at[mine], parents.at[mine, my_wide], parent_sent, parent_sem, (w, mine)).start()
-
-    pltpu.make_async_copy(parent.at[mine], parents.at[mine, my_wide], parent_sem).start()
+    for step in range(blocks):
+        for core in (other, mine) if step else (other,):
+            remote(
+                parent.at[core],
+                parents.at[mine, my_block],
+                parent_sent,
+                parent_sem,
+                (across(step), core),
+            ).start()
+    pltpu.make_async_copy(parent.at[mine], parents.at[mine, my_block], parent_sem).start()
 
     load.wait()
     side = min(256, buckets)
@@ -319,6 +323,19 @@
             arrived = utility.at[step, player, :, :, lanes]
             if forward:
                 wait_bytes(arrived, sums_sem.at[step, block])
+
+                @pl.when(index == 0)
+                def _():
+                    for hop in range(1, blocks):
+                        mine_now = utility.at[step, mine, :, :, lanes_of(my_block)]
+                        remote(
+                            mine_now,
+                            mine_now,
+                            sums_sent.at[step, owners + hop],
+                            sums_sem.at[step, my_block],
+                            (across(hop), mine),
+                        ).start()
+
                 remote(
                     arrived, arrived, pass_sent.at[step, block], pass_sem.at[step, block], sibling
                 ).start()
@@ -366,11 +383,11 @@
         factor = jnp.where(player == 0, -SCALE, SCALE).astype(jnp.float32)
         values[step, target] = (running[...] * factor).astype(WIRE)
 
-    def send_part(step, target, w):
-        rows, lanes = place(w)
-        return (
-            values.at[step, target, rows, lanes],
-            parts.at[step, mine, my_wide],
+    def send_part(step, target, index):
+        w = across(index)
+        return remote(
+            values.at[step, target, :, lanes_of(lax.rem(w, blocks))],
+            parts.at[step, mine, my_block],
             parts_sent.at[step],
             parts_sem.at[step, mine],
             (w, target),
@@ -380,10 +397,8 @@
     for step in range(STEPS):
         answer(step, mine)
 
-        @pl.loop(0, wide)
-        def _(index):
-            w = lax.rem(my_wide + index, wide)
-            remote(*send_part(step, other, w)).start()
+        for index in range(blocks):
+            send_part(step, other, index).start()
 
         if step:
             update(step - 1, other, False)
@@ -391,45 +406,55 @@
             begin(other)
         answer(step, other)
 
-        @pl.loop(1, wide)
-        def _(index):
-            w = lax.rem(my_wide + index, wide)
-            remote(*send_part(step, mine, w)).start()
-
-        own = values.at[step, mine, my_rows, my_lanes]
+        for index in range(1, blocks):
+            send_part(step, mine, index).start()
+        own = values.at[step, mine, :, lanes_of(my_block)]
         pltpu.make_async_copy(
-            own, parts.at[step, mine, my_wide], parts_sem.at[step, mine]
+            own, parts.at[step, mine, my_block], parts_sem.at[step, mine]
         ).start()
         finish_fold()
         mass[...] = jnp.zeros_like(mass)
         if step == 0:
             wait_bytes(parents, parent_sem)
-        totals = (jnp.zeros((ROWS, LANES), jnp.float32),) * lines
+        totals = [None] * lines
         for core in (other, mine):
             wait_bytes(parts.at[step, core], parts_sem.at[step, core])
-
-            def add(w, totals):
-                part = parts[step, core, w].astype(jnp.float32)
-                owner = jnp.broadcast_to(parents[core, w], (ROWS, LANES))
-                return tuple(
-                    total + jnp.where(owner == line, part, 0.0)
-                    for line, total in enumerate(totals)
-                )
-
-            totals = lax.fori_loop(0, wide, add, totals, unroll=8)
+            for column in range(blocks):
+                part = parts[step, core, column].astype(jnp.float32)
+                owner = jnp.broadcast_to(parents[core, column][:, :1], (beliefs, span))
+                for line in range(lines):
+                    term = jnp.where(owner == line, part, 0.0)
+                    totals[line] = term if totals[line] is None else totals[line] + term
+        for row in range(owners):
+            top, left = row % halves * ROWS, row // halves * LANES
+            for line in range(lines):
+                partial[step, row, line] = totals[line][top : top + ROWS, left : left + LANES]
+        for index in range(1, owners):
+            w = along(index)
+            remote(
+                partial.at[step, lax.div(w, blocks)],
+                gathered.at[step, my_row],
+                partial_sent.at[step, index],
+                partial_sem.at[step],
+                (w, mine),
+            ).start()
+        pltpu.make_async_copy(
+            partial.at[step, my_row], gathered.at[step, my_row], partial_sem.at[step]
+        ).start()
+        wait_bytes(gathered.at[step], partial_sem.at[step])
         for line in range(lines):
-            sums[step, line] = totals[line].astype(WIRE)
+            total = gathered[step, 0, line]
+            for row in range(1, owners):
+                total = total + gathered[step, row, line]
+            sums[step, line] = total.astype(WIRE)
 
         here = utility.at[step, mine, :, my_rows, my_lanes]
-
-        @pl.loop(1, wide)
-        def _(index):
-            w = lax.rem(my_wide + index * toward + wide, wide)
+        arrival = sums_sem.at[step, my_block]
+        for index in range(1, owners):
             remote(
-                sums.at[step], here, sums_sent.at[step, index], sums_sem.at[step, my_block], (w, mine)
+                sums.at[step], here, sums_sent.at[step, index], arrival, (along(index), mine)
             ).start()
-
-        pltpu.make_async_copy(sums.at[step], here, sums_sem.at[step, my_block]).start()
+        pltpu.make_async_copy(sums.at[step], here, arrival).start()
         update(step, mine, True)
 
     final = STEPS - 1
@@ -450,19 +475,22 @@
     for copy in level_copies:
         copy.wait_send()
     pot_copy.wait_send()
-    for core, count in enumerate((wide, wide - 1)):
+    for core, count in enumerate((blocks, blocks - 1)):
         wait_bytes(parents.at[core, pl.ds(0, count)], parent_sent)
     for step in range(STEPS):
-        for core, count in enumerate((wide, wide - 1)):
+        for core, count in enumerate((blocks, blocks - 1)):
             wait_bytes(parts.at[step, core, pl.ds(0, count)], parts_sent.at[step])
+        for index in range(1, owners):
+            wait_bytes(partial.at[step, 0], partial_sent.at[step, index])
+            wait_bytes(sums.at[step], sums_sent.at[step, index])
+        for hop in range(1, blocks):
+            wait_bytes(
+                utility.at[step, mine, :, :, lanes_of(my_block)], sums_sent.at[step, owners + hop]
+            )
 
         @pl.loop(0, blocks)
         def _(block):
             wait_bytes(utility.at[step, mine, :, :, lanes_of(block)], pass_sent.at[step, block])
-
-        @pl.loop(1, wide)
-        def _(index):
-            wait_bytes(sums.at[step], sums_sent.at[step, index])
 
     for out in outs:
         out.wait()
@@ -475,6 +503,7 @@
     whole = (players, levels, lines, beliefs, buckets)
     tile = (ROWS, LANES)
     blocks = buckets // next(width for width in (SPAN, LANES) if buckets % width == 0)
+    owners = wide // blocks
     dma = pltpu.SemaphoreType.DMA
     return pl.pallas_call(
         functools.partial(solve_kernel, wide),
@@ -499,12 +528,14 @@
             pltpu.VMEM((2, buckets, buckets), jnp.bfloat16),
             pltpu.VMEM((levels, lines, 8, LANES), jnp.float32),
             pltpu.VMEM((players, 1, LANES), jnp.int32),
-            pltpu.VMEM((2, wide, 1, LANES), jnp.int32),
+            pltpu.VMEM((2, blocks, 1, LANES), jnp.int32),
             pltpu.VMEM((players, beliefs, buckets), jnp.bfloat16),
             pltpu.VMEM((players, levels, lines, beliefs, LANES), jnp.float32),
             pltpu.VMEM((players, levels, lines, beliefs, LANES), jnp.float32),
             pltpu.VMEM((STEPS, players, beliefs, buckets), WIRE),
-            pltpu.VMEM((STEPS, 2, wide) + tile, WIRE),
+            pltpu.VMEM((STEPS, 2, blocks, beliefs, buckets // blocks), WIRE),
+            pltpu.VMEM((STEPS, owners, lines) + tile, jnp.float32),
+            pltpu.VMEM((STEPS, owners, lines) + tile, jnp.float32),
             pltpu.VMEM((STEPS, lines) + tile, WIRE),
             pltpu.VMEM((STEPS, players, lines, beliefs, buckets), WIRE),
             pltpu.VMEM((players, lines, beliefs, buckets), jnp.float32),
@@ -518,8 +549,10 @@
             dma,
             dma((STEPS, 2)),
             dma((STEPS,)),
+            dma((STEPS,)),
+            dma((STEPS, owners)),
             dma((STEPS, blocks)),
-            dma((STEPS, wide)),
+            dma((STEPS, owners + blocks)),
             dma((STEPS, blocks)),
             dma((STEPS, blocks)),
             dma((2, 2)),

time: 54.8 us -> 65.2 us (1.19)
  Pallas kernels: 48.8 us -> 59.3 us
    pallas_call x1, Pallas kernels: 48.8 us -> 59.3 us  [solve(): pl.pallas_call(functools.partial(solve_kernel, wide), out_shape=(jax.Shap...]
where the time goes in v4:
time: 65.2 us; the launch traced here: 65 us
  Pallas kernels  59.3 us (91%)
  local copies, waits for them, and re-layouts  3.77 us (6%)
  between operations  1.93 us (3%)
    pallas_call x1, Pallas kernels, solve(): pl.pallas_call(functools.partial(solve_kernel, wide), out_shape=(jax.Shap...  59.3 us
    unnamed x2, local copies, waits for them, and re-layouts  3.77 us

profile of v4, /device:TPU:1, one launch (start us, length us, event | category | flops | bytes accessed | tf_op | source)
XLA Modules:
  0.0 65.0 jit_solution(4059420761406736814)
XLA Ops:
  1.9 59.3 %shard_map.68 = (f32[2,1,2,32,1024]{4,3,2,1,0:T(8,128)}, f32[2,2,32,1024]{3,2,1,0:T(8,128)}) custom-call(f32[2,1,2,32,1024]{4,3,2,1,0:T(8,128)} %logits_ref.1, f32[1,2]{1,0:T(1,128)} %pot_ref.1, bf16[1,1024,1024]{2,1,0:T(8,128)(2,1)} %payoff_ref.1, s32[1]{0:T(128)S(6)} %copy.9.first_ref, s32[1]{0:T(128)S(6)} %copy.10.second_ref), custom_call_target="tpu_custom_call" | custom-call | tf_op jit(solution)/shard_map/pallas_call | solution.py:508
  61.2 1.9 %copy.11 = f32[2,1,2,32,1024]{4,3,2,1,0:T(8,128)} copy(f32[2,1,2,32,1024]{4,3,2,1,0:T(8,128)} %get-tuple-element.4) | data formatting | bytes 1048576
  63.1 1.9 %copy.12 = f32[2,2,32,1024]{3,2,1,0:T(8,128)} copy(f32[2,2,32,1024]{3,2,1,0:T(8,128)} %get-tuple-element.5) | data formatting | bytes 1048576

commit v5 on v2

--- a/solution.py
+++ b/solution.py
@@ -189,8 +189,8 @@
     parent[1] = jnp.full((1, LANES), second_ref[0], jnp.int32)
     for level in range(own_levels):
         for line in range(lines):
-            pots[mine * own_levels + level, line] = jnp.broadcast_to(
-                pot_ref[level : level + 1, line : line + 1], (8, LANES)
+            pots[mine * own_levels + level, line] = jnp.full(
+                (8, LANES), pot_ref[level, line], jnp.float32
             )
     mass[...] = jnp.zeros_like(mass)
     pl.semaphore_wait(barrier, devices - 1)
@@ -437,7 +437,7 @@
         ),
         in_specs=[
             pl.BlockSpec(memory_space=pltpu.HBM),
-            pl.BlockSpec(memory_space=pltpu.VMEM),
+            pl.BlockSpec(memory_space=pltpu.SMEM),
             pl.BlockSpec(memory_space=pltpu.HBM),
             pl.BlockSpec(memory_space=pltpu.SMEM),
             pl.BlockSpec(memory_space=pltpu.SMEM),
@@ -477,7 +477,7 @@
             dma((2, 2)),
         ],
         compiler_params=pltpu.CompilerParams(
-            collective_id=0, has_side_effects=True, vmem_limit_bytes=32 * 1024 * 1024
+            collective_id=0, has_side_effects=True, vmem_limit_bytes=52 * 1024 * 1024
         ),
     )(plan_logits, pot_size, payoff_tiles, parent_first, parent_second)
 

time: 52.9 us -> 51.7 us (0.977)
  local copies, waits for them, and re-layouts: 4.87 us -> 3.28 us
    unnamed x8 -> x6, local copies, waits for them, and re-layouts: 4.87 us -> 3.28 us
where the time goes in v5:
time: 51.7 us; the launch traced here: 51.5 us
  Pallas kernels  46.3 us (90%)
  local copies, waits for them, and re-layouts  3.28 us (6%)
  between operations  1.94 us (4%)
    pallas_call x1, Pallas kernels, solve(): pl.pallas_call(functools.partial(solve_kernel, wide), out_shape=(jax.Shap...  46.3 us
    unnamed x6, local copies, waits for them, and re-layouts  3.28 us

profile of v5, /device:TPU:1, one launch (start us, length us, event | category | flops | bytes accessed | tf_op | source)
XLA Modules:
  0.0 51.5 jit_solution(7629927399748667478)
XLA Ops:
  1.9 0.0 copy-start
  1.9 1.0 %copy-done = f32[2,1,2,32,1024]{4,3,2,1,0:T(8,128)S(1)} copy-done((f32[2,1,2,32,1024]{4,3,2,1,0:T(8,128)S(1)}, f32[2,1,2,32,1024]{4,3,2,1,0:T(8,128)}, u32[]{:S(2)}) %copy-start) | copy-done | bytes 524312
  3.0 0.0 copy-start.1
  3.0 0.7 %copy-done.1 = f32[1,2]{1,0:T(1,128)S(1)} copy-done((f32[1,2]{1,0:T(1,128)S(1)}, f32[1,2]{1,0:T(1,128)}, u32[]{:S(2)}) %copy-start.1) | copy-done | bytes 32
  3.6 46.3 %shard_map.68 = (f32[2,1,2,32,1024]{4,3,2,1,0:T(8,128)S(1)}, f32[2,2,32,1024]{3,2,1,0:T(8,128)S(1)}) custom-call(f32[2,1,2,32,1024]{4,3,2,1,0:T(8,128)S(1)} %copy-done, f32[1,2]{1,0:T(1,128)S(1)} %copy-done.1, bf16[1,1024,1024]{2,1,0:T(8,128)(2,1)} %payoff_ref.1, s32[1]{0:T(128)S(6)} %copy.9.first_ref, s32[1]{0:T(128)S(6)} %copy.10.second_ref), custom_call_target="tpu_custom_call" | custom-call | tf_op jit(solution)/shard_map/pallas_call | solution.py:432
  49.9 0.8 %copy.11 = f32[2,1,2,32,1024]{4,3,2,1,0:T(8,128)} copy(f32[2,1,2,32,1024]{4,3,2,1,0:T(8,128)S(1)} %get-tuple-element.4) | data formatting | bytes 1048576
  50.7 0.8 %copy.12 = f32[2,2,32,1024]{3,2,1,0:T(8,128)} copy(f32[2,2,32,1024]{3,2,1,0:T(8,128)S(1)} %get-tuple-element.5) | data formatting | bytes 1048576
Async XLA Ops:
  1.9 1.0 %copy-start = (f32[2,1,2,32,1024]{4,3,2,1,0:T(8,128)S(1)}, f32[2,1,2,32,1024]{4,3,2,1,0:T(8,128)}, u32[]{:S(2)}) copy-start(f32[2,1,2,32,1024]{4,3,2,1,0:T(8,128)} %logits_ref.1) | copy-start | bytes 1572868
  3.0 0.7 %copy-start.1 = (f32[1,2]{1,0:T(1,128)S(1)}, f32[1,2]{1,0:T(1,128)}, u32[]{:S(2)}) copy-start(f32[1,2]{1,0:T(1,128)} %pot_ref.1) | copy-start | bytes 28
